TPU v7x, 32 devices: a whole 2x2x4 slice. The times are simulated.
32 devices in a mesh: dp: 2 (over y), expert: 16 (over z, x, core).
Axes of the slice: x: 2, y: 2, z: 4, core: 2. Of those that a mesh axis runs over, the one named last changes fastest.
Arguments:
- grad_out: bfloat16 [1024, 4096], P(('dp', 'expert')), may hold values from -6 to 6
- expert_ids: int32 [1024, 8], P(('dp', 'expert')), may hold values from 0 to 15, all different within a row; in each aligned block of 32 rows (0 to 31, 32 to 63, ...) at most 20 rows name the same one
- route_weights: float32 [1024, 8], P(('dp', 'expert')), may hold values from 0.02 to 0.2
- hidden_act: bfloat16 [2, 16, 320, 1536], P('dp', 'expert'), may hold values from -6 to 6
- projection: bfloat16 [16, 1536, 256], P('expert', 'dp'), may hold values from -0.15625 to 0.15625
Outputs:
- projected_grad: bfloat16 [16, 4096, 256], P('expert', 'dp')
Inputs may be any that keep to these rules, and one draw needn't show every extreme that they name: `expert_ids`: each row names 8 different experts. Among the 32 tokens of one device (aligned blocks of rows), no expert is named more than 20 times, a bound that some block reaches.
All inputs are finite; a program needn't handle non-finite values.
Results may differ from a plain program's by a relative error of at most 0.0058.
Values may be sent and summed in bfloat16 or wider, within the bound.
A program may use at most 64 MiB of HBM per device.

v0:
```python
import jax
import jax.numpy as jnp
from jax import lax
from jax.sharding import PartitionSpec as P


def shards(grad_out, expert_ids, route_weights, hidden_act, projection):
    token_count = grad_out.shape[0]
    width = grad_out.shape[1]
    top_count = expert_ids.shape[1]
    expert_count = lax.axis_size("expert")
    slot_count = hidden_act.shape[2]
    capacity = slot_count // expert_count
    route_total = token_count * top_count
    routed = expert_ids.reshape(-1)
    onehot = (routed[:, None] == jnp.arange(expert_count, dtype=jnp.int32)[None, :]).astype(
        jnp.int32
    )
    earlier = jnp.cumsum(onehot, axis=0) - onehot
    position = jnp.sum(earlier * onehot, axis=1)
    slot = routed * capacity + position
    table = jnp.full((expert_count * capacity,), -1, jnp.int32)
    table = table.at[slot].set(jnp.arange(route_total, dtype=jnp.int32))
    valid = table >= 0
    picked = jnp.maximum(table, 0)
    rows = grad_out[picked // top_count].astype(jnp.float32)
    weight = route_weights.reshape(-1)[picked]
    weighted = jnp.where(valid[:, None], weight[:, None] * rows, 0.0).astype(jnp.bfloat16)
    outgoing = weighted.reshape(expert_count, capacity, width)
    hidden = hidden_act[0, 0]
    reduced = jnp.dot(
        hidden,
        lax.all_gather(projection[0], "dp", axis=0, tiled=True),
        preferred_element_type=jnp.float32,
    ).astype(jnp.bfloat16)
    arrived = lax.all_to_all(outgoing, "expert", split_axis=0, concat_axis=0, tiled=True).reshape(
        slot_count, width
    )
    share = lax.psum_scatter(
        lax.dot_general(
            arrived, reduced, (((0,), (0,)), ((), ())), preferred_element_type=jnp.float32
        ),
        "dp",
        scatter_dimension=0,
        tiled=True,
    )
    return share.astype(jnp.bfloat16)[None]


def solution(mesh):
    in_specs = (
        P(("dp", "expert"), None),
        P(("dp", "expert"), None),
        P(("dp", "expert"), None),
        P("dp", "expert", None, None),
        P("expert", "dp", None),
    )
    out_specs = P("expert", "dp", None)
    return jax.shard_map(shards, mesh=mesh, in_specs=in_specs, out_specs=out_specs, check_vma=False)
```

profile of v0, /device:TPU:1, one launch (start us, length us, event | category | flops | bytes accessed | tf_op | source)
XLA Modules:
  0.0 184.5 jit_solution(16391595456941839424)
XLA Ops:
  6.5 0.0 copy-start
  6.5 0.8 copy.7
  7.4 0.1 eq.29
  7.5 0.1 eq.25
  7.6 0.7 broadcast_multiply_fusion
  8.3 0.6 reduce-window.6
  8.8 0.2 slice_reduce_fusion
  9.1 0.1 copy.6
  9.1 0.1 mul.32
  9.2 0.1 fusion.7
  9.3 1.4 scatter_custom_fusion
  10.8 9.1 %gather_fusion.1 = bf16[320,4096]{1,0:T(8,128)(2,1)} fusion(bf16[32,4096]{1,0:T(8,128)(2,1)} %param.5, s32[1024]{0:T(1024)S(1)} %get-tuple-element.7), kind=kCustom, calls=%fused_computation.1 | custom fusion | bytes 5244160 | tf_op jit(solution)/shard_map/gather | solution.py:26
  19.9 0.0 copy-start.2
  19.9 5.0 %reshape.71 = f32[16,20,4096]{2,1,0:T(8,128)} reshape(bf16[320,4096]{1,0:T(8,128)(2,1)} %gather_fusion.1) | data formatting | bytes 7864320 | tf_op jit(solution)/shard_map/convert_element_type | solution.py:26
  24.9 0.0 copy-done.2
  24.9 0.1 copy.10
  24.9 0.1 reshape.69
  25.0 2.5 %gather_fusion = f32[320]{0:T(512)S(1)} fusion(f32[256]{0:T(256)S(1)} %reshape.69, s32[1024]{0:T(1024)S(1)} %get-tuple-element.8), kind=kCustom, calls=%fused_computation | custom fusion | bytes 3840 | tf_op jit(solution)/shard_map/gather | solution.py:27
  27.5 0.1 mul.34
  27.6 0.1 broadcast_in_dim.31
  27.7 5.6 %select_convert_fusion = bf16[16,20,4096]{2,1,0:T(8,128)(2,1)} fusion(f32[16,20,4096]{2,1,0:T(8,128)} %reshape.71, f32[16,20]{1,0:T(8,128)S(1)} %mul.34, pred[16,20]{1,0:T(8,128)(4,1)S(1)} %broadcast_in_dim.31), kind=kLoop, calls=%fused_computation.3 | loop fusion | flops 3932160 | bytes 7865920 | tf_op jit(solution)/shard_map/convert_element_type | solution.py:28
  33.3 0.0 copy-start.1
  33.3 7.5 %all-to-all-start = ((bf16[16,20,4096]{2,1,0:T(8,128)(2,1)}), bf16[16,20,4096]{2,1,0:T(8,128)(2,1)}, u32[]{:S(2)}, u32[]{:S(2)}) async-start(bf16[16,20,4096]{2,1,0:T(8,128)(2,1)} %select_convert_fusion), calls=%async_computation | async-start | bytes 6291456 | tf_op jit(solution)/shard_map/all_to_all | solution.py:36
  40.8 0.0 reduce-scatter.2.cloned.1.call-start
  40.8 0.0 copy-done.1
  40.8 11.4 %all-gather = bf16[1,1536,256]{2,1,0:T(8,128)(2,1)S(1)} all-gather(bf16[1,768,256]{2,1,0:T(8,128)(2,1)S(1)} %copy-done.1), channel_id=2, replica_groups=mesh['dp'=2,'expert'=16] {'dp'}, dimensions={1}, use_global_device_ids=true | all-gather | bytes 1179648 | tf_op jit(solution)/shard_map/all_gather | solution.py:33
  52.2 48.4 %all-to-all-done = bf16[16,20,4096]{2,1,0:T(8,128)(2,1)} async-done(((bf16[16,20,4096]{2,1,0:T(8,128)(2,1)}), bf16[16,20,4096]{2,1,0:T(8,128)(2,1)}, u32[]{:S(2)}, u32[]{:S(2)}) %all-to-all-start) | async-done | bytes 2621472 | tf_op jit(solution)/shard_map/all_to_all | solution.py:36
  100.6 4.3 %reshape.70 = bf16[320,4096]{1,0:T(8,128)(2,1)} reshape(bf16[16,20,4096]{2,1,0:T(8,128)(2,1)} %all-to-all-done) | data formatting | bytes 5242880 | tf_op jit(solution)/shard_map/reshape | solution.py:36
  104.9 0.0 copy-done
  104.9 5.8 %fusion = f32[4096,256]{1,0:T(8,128)} fusion(bf16[320,4096]{1,0:T(8,128)(2,1)} %reshape.70, bf16[1,1,320,1536]{3,2,1,0:T(8,128)(2,1)S(1)} %copy-done, bf16[1,1536,256]{2,1,0:T(8,128)(2,1)S(1)} %all-gather), kind=kOutput, calls=%fused_computation.5 | convolution fusion | flops 922828800 | bytes 8585216 | tf_op jit(solution)/shard_map/dot_general | solution.py:40
  110.7 0.0 reduce-scatter.2.cloned.1.call-update
  110.7 64.3 %reduce-scatter.2.cloned.1.call-done = f32[2048,256]{1,0:T(8,128)} async-done(((f32[4096,256]{1,0:T(8,128)}), f32[2048,256]{1,0:T(8,128)}) %reduce-scatter.2.cloned.1.call-update) | async-done | bytes 2097168 | tf_op jit(solution)/shard_map/reduce_scatter | solution.py:39
  175.0 2.7 %convert_bitcast_fusion = bf16[1,2048,256]{2,1,0:T(8,128)(2,1)} fusion(f32[2048,256]{1,0:T(8,128)} %reduce-scatter.2.cloned.1.call-done), kind=kLoop, calls=%fused_computation.6 | loop fusion | flops 524288 | bytes 3145728 | tf_op jit(solution)/shard_map/broadcast_in_dim | solution.py:47
  (8 shorter events, 0.1 us)
Async XLA Ops:
  6.5 98.4 %copy-start = (bf16[1,1,320,1536]{3,2,1,0:T(8,128)(2,1)S(1)}, bf16[1,1,320,1536]{3,2,1,0:T(8,128)(2,1)}, u32[]{:S(2)}) copy-start(bf16[1,1,320,1536]{3,2,1,0:T(8,128)(2,1)} %param.8) | copy-start | bytes 2949124
  19.9 5.0 %copy-start.2 = (f32[32,8]{0,1:T(8,128)S(1)}, f32[32,8]{0,1:T(8,128)}, u32[]{:S(2)}) copy-start(f32[32,8]{0,1:T(8,128)} %param.7) | copy-start | bytes 3076
  33.3 7.5 %copy-start.1 = (bf16[1,768,256]{2,1,0:T(8,128)(2,1)S(1)}, bf16[1,768,256]{2,1,0:T(8,128)(2,1)}, u32[]{:S(2)}) copy-start(bf16[1,768,256]{2,1,0:T(8,128)(2,1)} %param.9) | copy-start | bytes 1179652
  33.3 67.3 %all-to-all-start = ((bf16[16,20,4096]{2,1,0:T(8,128)(2,1)}), bf16[16,20,4096]{2,1,0:T(8,128)(2,1)}, u32[]{:S(2)}, u32[]{:S(2)}) async-start(bf16[16,20,4096]{2,1,0:T(8,128)(2,1)} %select_convert_fusion), calls=%async_computation | async-start | bytes 6291456 | tf_op jit(solution)/shard_map/all_to_all | solution.py:36
  40.8 134.3 %reduce-scatter.2.cloned.1.call-start = ((), (), s32[]{:S(2)}) async-start(), calls=%async_computation.2 | async-start | bytes 6291456 | tf_op jit(solution)/shard_map/reduce_scatter | solution.py:39
Sparse Core Ops, SparseCore 0:
  110.9 64.1 reduce-scatter.1
where the time goes:
time: 186 us; the launch traced here: 185 us
  waiting for transfers between devices  113 us (61%)
  local copies, waits for them, and re-layouts  23.9 us (13%)
  between operations  13.5 us (7%)
  blocking collectives  11.4 us (6%)
  other arithmetic  9.74 us (5%)
  starting transfers between devices  7.49 us (4%)
  matrix products  5.81 us (3%)
    reduce_scatter x1, waiting for transfers between devices, shards(): lax.psum_scatter(lax.dot_general(arrived, reduced, (((0,), (0,)), ((), ()...  64.3 us
    all_to_all x1, waiting for transfers between devices, shards(): lax.all_to_all(outgoing, 'expert', split_axis=0, concat_axis=0, tiled=True)  48.4 us
    all_gather x1, blocking collectives, shards(): lax.all_gather(projection[0], 'dp', axis=0, tiled=True)  11.4 us
    gather x1, local copies, waits for them, and re-layouts, shards(): rows = grad_out[picked // top_count].astype(jnp.float32)  9.1 us
    all_to_all x1, starting transfers between devices, shards(): lax.all_to_all(outgoing, 'expert', split_axis=0, concat_axis=0, tiled=True)  7.45 us
    dot_general x1, matrix products, shards(): lax.dot_general(arrived, reduced, (((0,), (0,)), ((), ())), preferred_ele...  5.81 us
    convert_element_type x1, other arithmetic, shards(): jnp.where(valid[:, None], weight[:, None] * rows, 0.0).astype(jnp.bfloat16)  5.64 us
    convert_element_type x1, local copies, waits for them, and re-layouts, shards(): rows = grad_out[picked // top_count].astype(jnp.float32)  4.96 us
  transfers between devices with their start and end apart: 2, of which 2 were waited for; matrix products, arithmetic and copies ran while one was open for 0% of the time, Pallas kernels for 0%

commit v1 on v0

v1 whole, which is shorter than its diff:
```python
import functools

import jax
import jax.numpy as jnp
from jax import lax
from jax.experimental import pallas as pl
from jax.experimental.pallas import tpu as pltpu
from jax.sharding import PartitionSpec as P

MESH = pl.DeviceIdType.MESH
PLANE = 4
TO_Y, TO_X, TO_UP, TO_DOWN, TO_CORE, TO_PAIR = range(6)


def gather_kernel(
    nz,
    g_ref, ids_ref, w_ref, h_ref, p_ref,
    out_ref,
    gbuf, msgs, meta, hbuf, pf, rt,
    send, recv, meta_send, meta_recv, side_send, side_recv, local,
):
    experts = nz * PLANE
    tokens = g_ref.shape[0]
    half = gbuf.shape[2]
    slots = hbuf.shape[0]
    capacity = slots // experts
    y = lax.axis_index("dp")
    me = lax.axis_index("expert")
    core = lax.rem(me, 2)
    x = lax.rem(lax.div(me, 2), 2)
    z = lax.div(me, PLANE)
    peer = 1 - y
    pair = z + 1 - 2 * lax.rem(z, 2)

    def place(ys, zs, xs, cs):
        return zs * (2 * PLANE) + ys * PLANE + xs * 2 + cs

    def device(zs, xs, cs):
        return (y, zs * PLANE + xs * 2 + cs)

    barrier = pltpu.get_barrier_semaphore()
    pl.semaphore_signal(barrier, inc=1, device_id=(peer, me), device_id_type=MESH)
    for k in range(1, experts):
        pl.semaphore_signal(
            barrier, inc=1, device_id=(y, lax.rem(me + k, experts)), device_id_type=MESH
        )

    own_columns = pl.ds(pl.multiple_of(y * half, half), half)
    peer_columns = pl.ds(pl.multiple_of(peer * half, half), half)
    own_place = place(y, z, x, core)
    copies = [
        pltpu.make_async_copy(g_ref.at[:, own_columns], gbuf.at[own_place], local.at[0]),
        pltpu.make_async_copy(h_ref.at[0, 0], hbuf, local.at[1]),
        pltpu.make_async_copy(p_ref.at[0], pf.at[y], local.at[2]),
    ]
    for copy in copies:
        copy.start()

    ids = jnp.concatenate([ids_ref[...]] * PLANE, axis=1)
    gains = jnp.concatenate([w_ref[...]] * PLANE, axis=1)
    expert_row = lax.broadcasted_iota(jnp.int32, (experts, 128), 0)
    weight = jnp.zeros((experts, 128), jnp.float32)
    named = jnp.zeros((experts, 128), jnp.float32)
    for k in range(ids_ref.shape[0]):
        hit = ids[k : k + 1] == expert_row
        weight = weight + jnp.where(hit, gains[k : k + 1], 0.0)
        named = named + jnp.where(hit, 1.0, 0.0)
    first = lax.broadcasted_iota(jnp.int32, (128, 128), 0)
    second = lax.broadcasted_iota(jnp.int32, (128, 128), 1)
    earlier = jnp.logical_and(first < second, first >= second - lax.rem(second, tokens))
    position = jnp.dot(
        named.astype(jnp.bfloat16),
        jnp.where(earlier, 1.0, 0.0).astype(jnp.bfloat16),
        preferred_element_type=jnp.float32,
    )
    base = (me * capacity + 1).astype(jnp.float32)
    number = jnp.where(named > 0.5, position + base, 0.0)
    lane_group = lax.div(lax.broadcasted_iota(jnp.int32, (experts, 128), 1), tokens)
    mine = lane_group == lax.rem(me, PLANE)
    msgs[:, 0, :] = jnp.where(mine, weight, 0.0)
    msgs[:, 1, :] = jnp.where(mine, number, 0.0)
    meta[pl.ds(me, 1)] = msgs[pl.ds(me, 1)]

    pl.semaphore_wait(barrier, experts)

    pending = []

    def send_block(src, where, way, target, condition=None):
        copy = pltpu.make_async_remote_copy(
            src_ref=src,
            dst_ref=gbuf.at[where],
            send_sem=send.at[way, where],
            recv_sem=recv.at[where],
            device_id=target,
            device_id_type=MESH,
        )
        pending.append((condition, copy))
        if condition is None:
            copy.start()
        else:
            pl.when(condition)(copy.start)

    def arrived(where):
        pltpu.make_async_remote_copy(
            src_ref=gbuf.at[where],
            dst_ref=gbuf.at[where],
            send_sem=send.at[0, where],
            recv_sem=recv.at[where],
            device_id=(peer, me),
            device_id_type=MESH,
        ).wait_recv()

    def both(a, b):
        return b if a is None else jnp.logical_and(a, b)

    to_x = device(z, 1 - x, core)
    to_core = device(z, x, 1 - core)
    to_up = device(lax.rem(z + 1, nz), x, core)
    to_down = device(lax.rem(z + nz - 1, nz), x, core)
    to_pair = device(pair, x, core)

    def side_copy(index, src, dst):
        return pltpu.make_async_remote_copy(
            src_ref=src, dst_ref=dst, send_sem=side_send.at[index], recv_sem=side_recv.at[index],
            device_id=(peer, me), device_id_type=MESH,
        )

    own = g_ref.at[:, own_columns]
    send_block(g_ref.at[:, peer_columns], own_place, TO_Y, (peer, me))
    send_block(own, own_place, TO_X, to_x)
    send_block(own, own_place, TO_UP, to_up, z < nz - 1)
    send_block(own, own_place, TO_DOWN, to_down, z > 0)
    send_block(own, own_place, TO_CORE, to_core)
    basis = side_copy(0, p_ref.at[0], pf.at[y])
    basis.start()
    notes = []
    for k in range(1, experts):
        target = lax.rem(me + k, experts)
        note = pltpu.make_async_remote_copy(
            src_ref=msgs.at[target], dst_ref=meta.at[me],
            send_sem=meta_send.at[k], recv_sem=meta_recv.at[me],
            device_id=(y, target), device_id_type=MESH,
        )
        note.start()
        notes.append(note)

    where = place(peer, z, x, core)
    arrived(where)
    block = gbuf.at[where]
    send_block(block, where, TO_X, to_x)
    send_block(block, where, TO_UP, to_up, z < nz - 1)
    send_block(block, where, TO_DOWN, to_down, z > 0)
    send_block(block, where, TO_CORE, to_core)

    def sides(distance):
        below = (z - distance, z - distance >= 0, TO_UP, to_up, z < nz - 1)
        above = (z + distance, z + distance < nz, TO_DOWN, to_down, z > 0)
        return below, above

    def from_column(distance, same):
        ys = y if same else peer
        for zs, valid, way, target, further in sides(distance):
            where = place(ys, zs, x, core)
            pl.when(valid)(functools.partial(arrived, where))
            block = gbuf.at[where]
            if distance < nz - 1:
                send_block(block, where, way, target, both(valid, further))
            crossing = valid
            if same and distance == 1:
                crossing = both(valid, zs != pair)
            send_block(block, where, TO_X, to_x, crossing)
            send_block(block, where, TO_CORE, to_core, valid)

    def from_x(distance, same):
        ys = y if same else peer
        if distance == 0:
            where = place(ys, z, 1 - x, core)
            arrived(where)
            if same:
                send_block(gbuf.at[where], where, TO_PAIR, to_pair)
            send_block(gbuf.at[where], where, TO_CORE, to_core)
            return
        for zs, valid, _, _, _ in sides(distance):
            if same and distance == 1:
                valid = both(valid, zs != pair)
            where = place(ys, zs, 1 - x, core)
            pl.when(valid)(functools.partial(arrived, where))
            send_block(gbuf.at[where], where, TO_CORE, to_core, valid)

    def from_pair():
        where = place(y, pair, 1 - x, core)
        arrived(where)
        send_block(gbuf.at[where], where, TO_CORE, to_core)

    def reduce_rows():
        for k in range(1, experts):
            source = lax.rem(me + k, experts)
            pltpu.make_async_remote_copy(
                src_ref=msgs.at[source], dst_ref=meta.at[source],
                send_sem=meta_send.at[k], recv_sem=meta_recv.at[source],
                device_id=(y, source), device_id_type=MESH,
            ).wait_recv()
        copies[1].wait()
        copies[2].wait()
        basis.wait_recv()
        depth = pf.shape[1]
        reduced = jnp.dot(
            hbuf[:, :depth], pf[0], preferred_element_type=jnp.float32
        ) + jnp.dot(hbuf[:, depth:], pf[1], preferred_element_type=jnp.float32)
        turned = reduced.T.astype(jnp.bfloat16)
        slot = lax.broadcasted_iota(jnp.int32, (slots, 128), 0).astype(jnp.float32) + 1.0
        for zs in range(nz):
            rows = jnp.sum(meta[PLANE * zs : PLANE * (zs + 1)], axis=0)
            chosen = jnp.where(slot == rows[1:2], 1.0, 0.0).astype(jnp.bfloat16)
            picked = jnp.dot(turned, chosen, preferred_element_type=jnp.float32)
            rt[y, zs] = (picked * rows[0:1]).astype(jnp.bfloat16)

    from_x(0, True)
    from_column(1, True)
    from_x(0, False)
    from_column(1, False)
    from_x(1, True)
    from_column(2, True)
    from_x(1, False)
    from_column(2, False)
    reduce_rows()
    factors = side_copy(1, rt.at[y], rt.at[y])
    factors.start()
    from_x(2, True)
    from_column(3, True)
    from_x(2, False)
    from_column(3, False)
    from_pair()
    from_x(3, True)
    from_x(3, False)

    copies[0].wait()
    factors.wait_recv()
    for xs in range(2):
        for ys in range(2):
            for zs in range(nz):
                arrived(place(ys, zs, xs, 1 - core))

    left = jnp.concatenate(
        [rt[ys, zs] for zs in range(nz) for ys in range(2)], axis=1
    )
    width = 512

    def columns_body(i, carry):
        columns = pl.ds(pl.multiple_of(i * width, width), width)
        right = gbuf[:, :, columns].reshape(gbuf.shape[0] * tokens, width)
        out_ref[:, columns] = jnp.dot(
            left, right, preferred_element_type=jnp.float32
        ).astype(jnp.bfloat16)
        return carry

    lax.fori_loop(0, half // width, columns_body, 0)

    for condition, copy in pending:
        if condition is None:
            copy.wait_send()
        else:
            pl.when(condition)(copy.wait_send)
    for copy in [basis, factors, *notes]:
        copy.wait_send()


def gathered(grad_out, expert_ids, route_weights, hidden_act, projection):
    experts = lax.axis_size("expert")
    nz = experts // PLANE
    tokens, features = grad_out.shape
    half = features // 2
    slots, hidden = hidden_act.shape[2:]
    rank = projection.shape[2]
    vmem = pl.BlockSpec(memory_space=pltpu.VMEM)
    anywhere = pl.BlockSpec(memory_space=pl.ANY)
    blocks = 2 * experts
    out = pl.pallas_call(
        functools.partial(gather_kernel, nz),
        out_shape=jax.ShapeDtypeStruct((rank, half), jnp.bfloat16),
        in_specs=[anywhere, vmem, vmem, anywhere, anywhere],
        out_specs=vmem,
        scratch_shapes=[
            pltpu.VMEM((blocks, tokens, half), jnp.bfloat16),
            pltpu.VMEM((experts, 2, 128), jnp.float32),
            pltpu.VMEM((experts, 2, 128), jnp.float32),
            pltpu.VMEM((slots, hidden), jnp.bfloat16),
            pltpu.VMEM((2, hidden // 2, rank), jnp.bfloat16),
            pltpu.VMEM((2, nz, rank, PLANE * tokens), jnp.bfloat16),
            pltpu.SemaphoreType.DMA((6, blocks)),
            pltpu.SemaphoreType.DMA((blocks,)),
            pltpu.SemaphoreType.DMA((experts,)),
            pltpu.SemaphoreType.DMA((experts,)),
            pltpu.SemaphoreType.DMA((2,)),
            pltpu.SemaphoreType.DMA((2,)),
            pltpu.SemaphoreType.DMA((3,)),
        ],
        compiler_params=pltpu.CompilerParams(
            collective_id=0, has_side_effects=True, vmem_limit_bytes=60 * 1024 * 1024
        ),
        cost_estimate=pl.CostEstimate(
            flops=2 * rank * (half * blocks * tokens + slots * hidden),
            bytes_accessed=4 * 1024 * 1024,
            transcendentals=0,
        ),
        name="gather_project",
    )(grad_out, expert_ids.T, route_weights.T, hidden_act, projection)
    return out.T[None]


def exchanged(grad_out, expert_ids, route_weights, hidden_act, projection):
    token_count, width = grad_out.shape
    top_count = expert_ids.shape[1]
    expert_count = lax.axis_size("expert")
    slot_count = hidden_act.shape[2]
    capacity = slot_count // expert_count
    onehot = (
        expert_ids[:, :, None] == jnp.arange(expert_count, dtype=jnp.int32)
    ).astype(jnp.float32)
    named = jnp.sum(onehot, axis=1)
    order = jnp.arange(token_count)
    before = (order[:, None] > order[None, :]).astype(jnp.float32)
    earlier = jnp.dot(before, named, preferred_element_type=jnp.float32)
    position = jnp.sum(onehot * earlier[:, None, :], axis=2).astype(jnp.int32)
    slot = (expert_ids * capacity + position).reshape(-1)
    table = jnp.full((expert_count * capacity,), -1, jnp.int32)
    table = table.at[slot].set(jnp.arange(token_count * top_count, dtype=jnp.int32))
    picked = jnp.maximum(table, 0)
    rows = grad_out[picked // top_count].astype(jnp.float32)
    weight = route_weights.reshape(-1)[picked]
    weighted = jnp.where((table >= 0)[:, None], weight[:, None] * rows, 0.0)
    outgoing = weighted.astype(jnp.bfloat16).reshape(expert_count, capacity, width)
    reduced = jnp.dot(
        hidden_act[0, 0],
        lax.all_gather(projection[0], "dp", axis=0, tiled=True),
        preferred_element_type=jnp.float32,
    ).astype(jnp.bfloat16)
    arrived = lax.all_to_all(outgoing, "expert", split_axis=0, concat_axis=0, tiled=True)
    share = lax.psum_scatter(
        lax.dot_general(
            arrived.reshape(slot_count, width),
            reduced,
            (((0,), (0,)), ((), ())),
            preferred_element_type=jnp.float32,
        ),
        "dp",
        scatter_dimension=0,
        tiled=True,
    )
    return share.astype(jnp.bfloat16)[None]


def solution(mesh):
    in_specs = (
        P(("dp", "expert"), None),
        P(("dp", "expert"), None),
        P(("dp", "expert"), None),
        P("dp", "expert", None, None),
        P("expert", "dp", None),
    )
    out_specs = P("expert", "dp", None)
    small = mesh.shape["dp"] == 2 and mesh.shape["expert"] == 16
    return jax.shard_map(
        gathered if small else exchanged,
        mesh=mesh, in_specs=in_specs, out_specs=out_specs, check_vma=False,
    )
```

time: 186 us -> 43.1 us (0.23)
  waiting for transfers between devices: 113 us -> 0 us
  Pallas kernels: 0 us -> 40.6 us
  local copies, waits for them, and re-layouts: 23.9 us -> 2.26 us
  between operations: 13.5 us -> 0.01 us
  blocking collectives: 11.4 us -> 0 us
  other arithmetic: 9.74 us -> 0 us
  starting transfers between devices: 7.49 us -> 0 us
  matrix products: 5.81 us -> 0 us
    reduce_scatter x1 -> x0, waiting for transfers between devices: 64.3 us -> none  [shards(): lax.psum_scatter(lax.dot_general(arrived, reduced, (((0,), (0,)), ((), ()...]
    all_to_all x1 -> x0, waiting for transfers between devices: 48.4 us -> none  [shards(): lax.all_to_all(outgoing, 'expert', split_axis=0, concat_axis=0, tiled=True)]
    pallas_call x0 -> x1, Pallas kernels: none -> 40.6 us  [gathered(): pl.pallas_call(functools.partial(gather_kernel, nz), out_shape=jax.ShapeD...]
    gather x2 -> x0, local copies, waits for them, and re-layouts: 11.6 us -> none  [the longest x1 9.1 us: shards(): rows = grad_out[picked // top_count].astype(jnp.float32)]
    all_gather x1 -> x0, blocking collectives: 11.4 us -> none  [shards(): lax.all_gather(projection[0], 'dp', axis=0, tiled=True)]
    all_to_all x1 -> x0, starting transfers between devices: 7.45 us -> none  [shards(): lax.all_to_all(outgoing, 'expert', split_axis=0, concat_axis=0, tiled=True)]
    dot_general x1 -> x0, matrix products: 5.81 us -> none  [shards(): lax.dot_general(arrived, reduced, (((0,), (0,)), ((), ())), preferred_ele...]
    convert_element_type x2 -> x0, other arithmetic: 5.65 us -> none  [the longest x1 5.64 us: shards(): jnp.where(valid[:, None], weight[:, None] * rows, 0.0).astype(jnp.bfloat16)]
  transfers between devices with their start and end apart: 2 -> 0, of which waited for: 2 -> 0; matrix products, arithmetic and copies ran while one was open for 0% -> 0% of each run, Pallas kernels for 0% -> 0%
where the time goes in v1:
time: 43.1 us; the launch traced here: 42.9 us
  Pallas kernels  40.6 us (94%)
  local copies, waits for them, and re-layouts  2.26 us (5%)
    pallas_call x1, Pallas kernels, gathered(): pl.pallas_call(functools.partial(gather_kernel, nz), out_shape=jax.ShapeD...  40.6 us
    broadcast_in_dim x1, local copies, waits for them, and re-layouts, gathered(): return out.T[None]  2.26 us

profile of v1, /device:TPU:1, one launch (start us, length us, event | category | flops | bytes accessed | tf_op | source)
XLA Modules:
  0.0 42.9 jit_solution(10361933793160618496)
XLA Ops:
  0.0 40.6 %gather_project.1 = bf16[256,2048]{1,0:T(8,128)(2,1)} custom-call(bf16[32,4096]{1,0:T(8,128)(2,1)} %g_ref.1, s32[8,32]{1,0:T(8,128)} %bitcast.6, f32[8,32]{1,0:T(8,128)} %bitcast.7, bf16[1,1,320,1536]{3,2,1,0:T(8,128)(2,1)} %h_ref.1, bf16[1,768,256]{2,1,0:T(8,128)(2,1)} %p_ref.1), custom_call_target="tpu_custom_call" | custom-call | flops 1325400064 | bytes 4194304 | tf_op jit(solution)/shard_map/gather_project/pallas_call | solution.py:278
  40.6 2.3 %copy.6 = bf16[1,2048,256]{2,1,0:T(8,128)(2,1)} copy(bf16[1,2048,256]{1,2,0:T(8,128)(2,1)} %bitcast.5) | data formatting | bytes 2097152 | tf_op jit(solution)/shard_map/broadcast_in_dim | solution.py:308

commit v2 on v1

v2 whole, which is shorter than its diff:
```python
import functools

import jax
import jax.numpy as jnp
from jax import lax
from jax.experimental import pallas as pl
from jax.experimental.pallas import tpu as pltpu
from jax.sharding import PartitionSpec as P

MESH = pl.DeviceIdType.MESH
PLANE = 4
PARTS, LAG, PAIR_AT, REDUCE_AT = 1, 2, 6, 5
TO_Y, TO_X, TO_UP, TO_DOWN, TO_CORE, TO_PAIR = range(6)


def gather_kernel(
    nz,
    g_ref, ids_ref, w_ref, h_ref, p_ref,
    out_ref,
    gbuf, msgs, meta, hbuf, pf, rt,
    send, recv, meta_send, meta_recv, side_send, side_recv, local,
):
    experts = nz * PLANE
    tokens = g_ref.shape[0]
    piece = gbuf.shape[3]
    slots = hbuf.shape[0]
    capacity = slots // experts
    y = lax.axis_index("dp")
    me = lax.axis_index("expert")
    core = lax.rem(me, 2)
    x = lax.rem(lax.div(me, 2), 2)
    z = lax.div(me, PLANE)
    peer = 1 - y
    pair = z + 1 - 2 * lax.rem(z, 2)

    def place(ys, zs, xs, cs):
        return zs * (2 * PLANE) + ys * PLANE + xs * 2 + cs

    def device(zs, xs, cs):
        return (y, zs * PLANE + xs * 2 + cs)

    barrier = pltpu.get_barrier_semaphore()
    pl.semaphore_signal(barrier, inc=1, device_id=(peer, me), device_id_type=MESH)
    for k in range(1, experts):
        pl.semaphore_signal(
            barrier, inc=1, device_id=(y, lax.rem(me + k, experts)), device_id_type=MESH
        )

    own_place = place(y, z, x, core)

    def columns_of(replica, part):
        return pl.ds(pl.multiple_of(replica * (PARTS * piece) + part * piece, piece), piece)

    copies = [
        pltpu.make_async_copy(h_ref.at[0, 0], hbuf, local.at[0]),
        pltpu.make_async_copy(p_ref.at[0], pf.at[y], local.at[1]),
    ]
    for part in range(PARTS):
        copies.append(
            pltpu.make_async_copy(
                g_ref.at[:, columns_of(y, part)], gbuf.at[part, own_place], local.at[2 + part]
            )
        )
    for copy in copies:
        copy.start()

    pl.semaphore_wait(barrier, experts)

    pending = []

    def send_block(src, where, part, way, target, condition=None):
        copy = pltpu.make_async_remote_copy(
            src_ref=gbuf.at[part, where] if src is None else src,
            dst_ref=gbuf.at[part, where],
            send_sem=send.at[way, part, where],
            recv_sem=recv.at[part, where],
            device_id=target,
            device_id_type=MESH,
        )
        pending.append((condition, copy))
        if condition is None:
            copy.start()
        else:
            pl.when(condition)(copy.start)

    def arrived(where, part):
        pltpu.make_async_remote_copy(
            src_ref=gbuf.at[part, where],
            dst_ref=gbuf.at[part, where],
            send_sem=send.at[0, part, where],
            recv_sem=recv.at[part, where],
            device_id=(peer, me),
            device_id_type=MESH,
        ).wait_recv()

    def both(a, b):
        return b if a is None else jnp.logical_and(a, b)

    to_x = device(z, 1 - x, core)
    to_core = device(z, x, 1 - core)
    to_up = device(lax.rem(z + 1, nz), x, core)
    to_down = device(lax.rem(z + nz - 1, nz), x, core)
    to_pair = device(pair, x, core)

    def side_copy(index, src, dst):
        return pltpu.make_async_remote_copy(
            src_ref=src, dst_ref=dst, send_sem=side_send.at[index], recv_sem=side_recv.at[index],
            device_id=(peer, me), device_id_type=MESH,
        )

    basis = side_copy(0, p_ref.at[0], pf.at[y])
    factors = side_copy(1, rt.at[y], rt.at[y])
    def write_notes():
        ids = jnp.concatenate([ids_ref[...]] * PLANE, axis=1)
        gains = jnp.concatenate([w_ref[...]] * PLANE, axis=1)
        expert_row = lax.broadcasted_iota(jnp.int32, (experts, 128), 0)
        weight = jnp.zeros((experts, 128), jnp.float32)
        named = jnp.zeros((experts, 128), jnp.float32)
        for k in range(ids_ref.shape[0]):
            hit = ids[k : k + 1] == expert_row
            weight = weight + jnp.where(hit, gains[k : k + 1], 0.0)
            named = named + jnp.where(hit, 1.0, 0.0)
        first = lax.broadcasted_iota(jnp.int32, (128, 128), 0)
        second = lax.broadcasted_iota(jnp.int32, (128, 128), 1)
        earlier = jnp.logical_and(first < second, first >= second - lax.rem(second, tokens))
        position = jnp.dot(
            named.astype(jnp.bfloat16),
            jnp.where(earlier, 1.0, 0.0).astype(jnp.bfloat16),
            preferred_element_type=jnp.float32,
        )
        base = (me * capacity + 1).astype(jnp.float32)
        number = jnp.where(named > 0.5, position + base, 0.0)
        lane_group = lax.div(lax.broadcasted_iota(jnp.int32, (experts, 128), 1), tokens)
        mine = lane_group == lax.rem(me, PLANE)
        msgs[:, 0, :] = jnp.where(mine, weight, 0.0)
        msgs[:, 1, :] = jnp.where(mine, number, 0.0)
        meta[pl.ds(me, 1)] = msgs[pl.ds(me, 1)]

    notes = []

    def send_notes():
        for k in range(1, experts):
            target = lax.rem(me + k, experts)
            note = pltpu.make_async_remote_copy(
                src_ref=msgs.at[target], dst_ref=meta.at[me],
                send_sem=meta_send.at[k], recv_sem=meta_recv.at[me],
                device_id=(y, target), device_id_type=MESH,
            )
            note.start()
            notes.append(note)

    def sides(distance):
        below = (z - distance, z - distance >= 0, TO_UP, to_up, z < nz - 1)
        above = (z + distance, z + distance < nz, TO_DOWN, to_down, z > 0)
        return below, above

    def from_column(distance, same, part):
        ys = y if same else peer
        if distance == 0:
            where = place(ys, z, x, core)
            src = None
            if same:
                src = g_ref.at[:, columns_of(y, part)]
                send_block(g_ref.at[:, columns_of(peer, part)], where, part, TO_Y, (peer, me))
            else:
                arrived(where, part)
            send_block(src, where, part, TO_X, to_x)
            send_block(src, where, part, TO_UP, to_up, z < nz - 1)
            send_block(src, where, part, TO_DOWN, to_down, z > 0)
            send_block(src, where, part, TO_CORE, to_core)
            return
        for zs, valid, way, target, further in sides(distance):
            where = place(ys, zs, x, core)
            pl.when(valid)(functools.partial(arrived, where, part))
            if distance < nz - 1:
                send_block(None, where, part, way, target, both(valid, further))
            crossing = valid
            if same and distance == 1:
                crossing = both(valid, zs != pair)
            send_block(None, where, part, TO_X, to_x, crossing)
            send_block(None, where, part, TO_CORE, to_core, valid)

    def from_x(distance, same, part):
        ys = y if same else peer
        if distance == 0:
            where = place(ys, z, 1 - x, core)
            arrived(where, part)
            send_block(None, where, part, TO_CORE, to_core)
            return
        for zs, valid, _, _, _ in sides(distance):
            if same and distance == 1:
                valid = both(valid, zs != pair)
            where = place(ys, zs, 1 - x, core)
            pl.when(valid)(functools.partial(arrived, where, part))
            send_block(None, where, part, TO_CORE, to_core, valid)

    def to_neighbour_pair():
        for part in range(PARTS):
            send_block(None, place(y, z, 1 - x, core), part, TO_PAIR, to_pair)

    def from_pair():
        for part in range(PARTS):
            where = place(y, pair, 1 - x, core)
            arrived(where, part)
            send_block(None, where, part, TO_CORE, to_core)

    def reduce_rows():
        for k in range(1, experts):
            source = lax.rem(me + k, experts)
            pltpu.make_async_remote_copy(
                src_ref=msgs.at[source], dst_ref=meta.at[source],
                send_sem=meta_send.at[k], recv_sem=meta_recv.at[source],
                device_id=(y, source), device_id_type=MESH,
            ).wait_recv()
        copies[0].wait()
        copies[1].wait()
        basis.wait_recv()
        depth = pf.shape[1]
        reduced = jnp.dot(
            hbuf[:, :depth], pf[0], preferred_element_type=jnp.float32
        ) + jnp.dot(hbuf[:, depth:], pf[1], preferred_element_type=jnp.float32)
        turned = reduced.T.astype(jnp.bfloat16)
        slot = lax.broadcasted_iota(jnp.int32, (slots, 128), 0).astype(jnp.float32) + 1.0
        for zs in range(nz):
            rows = jnp.sum(meta[PLANE * zs : PLANE * (zs + 1)], axis=0)
            chosen = jnp.where(slot == rows[1:2], 1.0, 0.0).astype(jnp.bfloat16)
            picked = jnp.dot(turned, chosen, preferred_element_type=jnp.float32)
            rt[y, zs] = (picked * rows[0:1]).astype(jnp.bfloat16)

    steps = [
        (distance, same, part)
        for distance in range(nz)
        for same in (True, False)
        for part in range(PARTS)
    ]
    for i in range(len(steps) + LAG):
        if i < len(steps):
            from_column(*steps[i])
        if i >= LAG:
            from_x(*steps[i - LAG])
        if i == PARTS - 1:
            write_notes()
            send_notes()
        if i == 2 * PARTS - 1:
            basis.start()
        if i == PAIR_AT * PARTS:
            to_neighbour_pair()
        if i == REDUCE_AT * PARTS:
            reduce_rows()
            factors.start()
    from_pair()

    for copy in copies[2:]:
        copy.wait()
    factors.wait_recv()
    for part in range(PARTS):
        for xs in range(2):
            for ys in range(2):
                for zs in range(nz):
                    arrived(place(ys, zs, xs, 1 - core), part)

    left = jnp.concatenate(
        [rt[ys, zs] for zs in range(nz) for ys in range(2)], axis=1
    )
    width = 512
    for part in range(PARTS):

        def columns_body(i, carry, part=part):
            offset = pl.multiple_of(i * width, width)
            right = gbuf[part, :, :, pl.ds(offset, width)].reshape(-1, width)
            out_ref[:, pl.ds(part * piece + offset, width)] = jnp.dot(
                left, right, preferred_element_type=jnp.float32
            ).astype(jnp.bfloat16)
            return carry

        lax.fori_loop(0, piece // width, columns_body, 0)

    for condition, copy in pending:
        if condition is None:
            copy.wait_send()
        else:
            pl.when(condition)(copy.wait_send)
    for copy in [basis, factors, *notes]:
        copy.wait_send()


def gathered(grad_out, expert_ids, route_weights, hidden_act, projection):
    experts = lax.axis_size("expert")
    nz = experts // PLANE
    tokens, features = grad_out.shape
    half = features // 2
    slots, hidden = hidden_act.shape[2:]
    rank = projection.shape[2]
    vmem = pl.BlockSpec(memory_space=pltpu.VMEM)
    anywhere = pl.BlockSpec(memory_space=pl.ANY)
    blocks = 2 * experts
    out = pl.pallas_call(
        functools.partial(gather_kernel, nz),
        out_shape=jax.ShapeDtypeStruct((rank, half), jnp.bfloat16),
        in_specs=[anywhere, vmem, vmem, anywhere, anywhere],
        out_specs=vmem,
        scratch_shapes=[
            pltpu.VMEM((PARTS, blocks, tokens, half // PARTS), jnp.bfloat16),
            pltpu.VMEM((experts, 2, 128), jnp.float32),
            pltpu.VMEM((experts, 2, 128), jnp.float32),
            pltpu.VMEM((slots, hidden), jnp.bfloat16),
            pltpu.VMEM((2, hidden // 2, rank), jnp.bfloat16),
            pltpu.VMEM((2, nz, rank, PLANE * tokens), jnp.bfloat16),
            pltpu.SemaphoreType.DMA((6, PARTS, blocks)),
            pltpu.SemaphoreType.DMA((PARTS, blocks)),
            pltpu.SemaphoreType.DMA((experts,)),
            pltpu.SemaphoreType.DMA((experts,)),
            pltpu.SemaphoreType.DMA((2,)),
            pltpu.SemaphoreType.DMA((2,)),
            pltpu.SemaphoreType.DMA((2 + PARTS,)),
        ],
        compiler_params=pltpu.CompilerParams(
            collective_id=0, has_side_effects=True, vmem_limit_bytes=60 * 1024 * 1024
        ),
        cost_estimate=pl.CostEstimate(
            flops=2 * rank * (half * blocks * tokens + slots * hidden),
            bytes_accessed=4 * 1024 * 1024,
            transcendentals=0,
        ),
        name="gather_project",
    )(grad_out, expert_ids.T, route_weights.T, hidden_act, projection)
    return out.T[None]


def exchanged(grad_out, expert_ids, route_weights, hidden_act, projection):
    token_count, width = grad_out.shape
    top_count = expert_ids.shape[1]
    expert_count = lax.axis_size("expert")
    slot_count = hidden_act.shape[2]
    capacity = slot_count // expert_count
    onehot = (
        expert_ids[:, :, None] == jnp.arange(expert_count, dtype=jnp.int32)
    ).astype(jnp.float32)
    named = jnp.sum(onehot, axis=1)
    order = jnp.arange(token_count)
    before = (order[:, None] > order[None, :]).astype(jnp.float32)
    earlier = jnp.dot(before, named, preferred_element_type=jnp.float32)
    position = jnp.sum(onehot * earlier[:, None, :], axis=2).astype(jnp.int32)
    slot = (expert_ids * capacity + position).reshape(-1)
    table = jnp.full((expert_count * capacity,), -1, jnp.int32)
    table = table.at[slot].set(jnp.arange(token_count * top_count, dtype=jnp.int32))
    picked = jnp.maximum(table, 0)
    rows = grad_out[picked // top_count].astype(jnp.float32)
    weight = route_weights.reshape(-1)[picked]
    weighted = jnp.where((table >= 0)[:, None], weight[:, None] * rows, 0.0)
    outgoing = weighted.astype(jnp.bfloat16).reshape(expert_count, capacity, width)
    reduced = jnp.dot(
        hidden_act[0, 0],
        lax.all_gather(projection[0], "dp", axis=0, tiled=True),
        preferred_element_type=jnp.float32,
    ).astype(jnp.bfloat16)
    arrived = lax.all_to_all(outgoing, "expert", split_axis=0, concat_axis=0, tiled=True)
    share = lax.psum_scatter(
        lax.dot_general(
            arrived.reshape(slot_count, width),
            reduced,
            (((0,), (0,)), ((), ())),
            preferred_element_type=jnp.float32,
        ),
        "dp",
        scatter_dimension=0,
        tiled=True,
    )
    return share.astype(jnp.bfloat16)[None]


def solution(mesh):
    in_specs = (
        P(("dp", "expert"), None),
        P(("dp", "expert"), None),
        P(("dp", "expert"), None),
        P("dp", "expert", None, None),
        P("expert", "dp", None),
    )
    out_specs = P("expert", "dp", None)
    small = mesh.shape["dp"] == 2 and mesh.shape["expert"] == 16
    return jax.shard_map(
        gathered if small else exchanged,
        mesh=mesh, in_specs=in_specs, out_specs=out_specs, check_vma=False,
    )
```

time: 43.1 us -> 40.7 us (0.944)
  Pallas kernels: 40.6 us -> 38.2 us
    pallas_call x1, Pallas kernels: 40.6 us -> 38.2 us  [gathered(): pl.pallas_call(functools.partial(gather_kernel, nz), out_shape=jax.ShapeD...]
where the time goes in v2:
time: 40.7 us; the launch traced here: 40.5 us
  Pallas kernels  38.2 us (94%)
  local copies, waits for them, and re-layouts  2.26 us (6%)
    pallas_call x1, Pallas kernels, gathered(): pl.pallas_call(functools.partial(gather_kernel, nz), out_shape=jax.ShapeD...  38.2 us
    broadcast_in_dim x1, local copies, waits for them, and re-layouts, gathered(): return out.T[None]  2.26 us

profile of v2, /device:TPU:1, one launch (start us, length us, event | category | flops | bytes accessed | tf_op | source)
XLA Modules:
  0.0 40.5 jit_solution(13121442217913602190)
XLA Ops:
  0.0 38.2 %gather_project.1 = bf16[256,2048]{1,0:T(8,128)(2,1)} custom-call(bf16[32,4096]{1,0:T(8,128)(2,1)} %g_ref.1, s32[8,32]{1,0:T(8,128)} %bitcast.6, f32[8,32]{1,0:T(8,128)} %bitcast.7, bf16[1,1,320,1536]{3,2,1,0:T(8,128)(2,1)} %h_ref.1, bf16[1,768,256]{2,1,0:T(8,128)(2,1)} %p_ref.1), custom_call_target="tpu_custom_call" | custom-call | flops 1325400064 | bytes 4194304 | tf_op jit(solution)/shard_map/gather_project/pallas_call | solution.py:297
  38.2 2.3 %copy.6 = bf16[1,2048,256]{2,1,0:T(8,128)(2,1)} copy(bf16[1,2048,256]{1,2,0:T(8,128)(2,1)} %bitcast.5) | data formatting | bytes 2097152 | tf_op jit(solution)/shard_map/broadcast_in_dim | solution.py:327

commit v3 on v2

--- a/solution.py
+++ b/solution.py
@@ -164,9 +164,9 @@
                 send_block(g_ref.at[:, columns_of(peer, part)], where, part, TO_Y, (peer, me))
             else:
                 arrived(where, part)
-            send_block(src, where, part, TO_X, to_x)
             send_block(src, where, part, TO_UP, to_up, z < nz - 1)
             send_block(src, where, part, TO_DOWN, to_down, z > 0)
+            send_block(src, where, part, TO_X, to_x)
             send_block(src, where, part, TO_CORE, to_core)
             return
         for zs, valid, way, target, further in sides(distance):
@@ -262,7 +262,7 @@
     left = jnp.concatenate(
         [rt[ys, zs] for zs in range(nz) for ys in range(2)], axis=1
     )
-    width = 512
+    width = piece
     for part in range(PARTS):
 
         def columns_body(i, carry, part=part):

time: 40.7 us -> 40.2 us (0.988)
  Pallas kernels: 38.2 us -> 37.7 us
    pallas_call x1, Pallas kernels: 38.2 us -> 37.7 us  [gathered(): pl.pallas_call(functools.partial(gather_kernel, nz), out_shape=jax.ShapeD...]
where the time goes in v3:
time: 40.2 us; the launch traced here: 40 us
  Pallas kernels  37.7 us (94%)
  local copies, waits for them, and re-layouts  2.26 us (6%)
    pallas_call x1, Pallas kernels, gathered(): pl.pallas_call(functools.partial(gather_kernel, nz), out_shape=jax.ShapeD...  37.7 us
    broadcast_in_dim x1, local copies, waits for them, and re-layouts, gathered(): return out.T[None]  2.26 us

profile of v3, /device:TPU:1, one launch (start us, length us, event | category | flops | bytes accessed | tf_op | source)
XLA Modules:
  0.0 40.0 jit_solution(928760972794244375)
XLA Ops:
  0.0 37.7 %gather_project.1 = bf16[256,2048]{1,0:T(8,128)(2,1)} custom-call(bf16[32,4096]{1,0:T(8,128)(2,1)} %g_ref.1, s32[8,32]{1,0:T(8,128)} %bitcast.6, f32[8,32]{1,0:T(8,128)} %bitcast.7, bf16[1,1,320,1536]{3,2,1,0:T(8,128)(2,1)} %h_ref.1, bf16[1,768,256]{2,1,0:T(8,128)(2,1)} %p_ref.1), custom_call_target="tpu_custom_call" | custom-call | flops 1325400064 | bytes 4194304 | tf_op jit(solution)/shard_map/gather_project/pallas_call | solution.py:297
  37.7 2.3 %copy.6 = bf16[1,2048,256]{2,1,0:T(8,128)(2,1)} copy(bf16[1,2048,256]{1,2,0:T(8,128)(2,1)} %bitcast.5) | data formatting | bytes 2097152 | tf_op jit(solution)/shard_map/broadcast_in_dim | solution.py:327
